TPU v7x, 256 devices: a whole 4x4x8 slice. The times are simulated.
256 devices in a mesh: rep: 8 (over x, z_hi), ep: 32 (over y, z_lo, core).
Axes of the slice: x: 4, y: 4, z: 8 (z_hi: 2, z_lo: 4; z = z_hi * 4 + z_lo), core: 2. Of those that a mesh axis runs over, the one named last changes fastest.
Arguments:
- tokens: bfloat16 [5120, 7168], P('ep', 'rep'), may hold values from -6 to 6
- slot_ids: int32 [5120, 2], P('ep'), may hold values from 0 to 63, all different within a row; in each aligned block of 160 rows (0 to 159, 160 to 319, ...) at most 10 rows name the same one
- gate_weights_per_slot: float32 [5120, 2], P('ep'), may hold values from 0.1 to 1
- w_gate: bfloat16 [32, 7168, 2048], P('ep', None, 'rep'), may hold values from -0.0625 to 0.0625
- w_up: bfloat16 [32, 7168, 2048], P('ep', None, 'rep'), may hold values from -0.0625 to 0.0625
- w_down: bfloat16 [32, 2048, 7168], P('ep', 'rep'), may hold values from -0.1875 to 0.1875
Outputs:
- moe_output: bfloat16 [5120, 7168], P('ep', 'rep')
Inputs may be any that keep to these rules, and one draw needn't show every extreme that they name: `slot_ids`: in each aligned block of 160 rows (the tokens of one index of ep) no slot is named by more than 10 rows, a bound that some block reaches; the 2 slots of a row differ.
All inputs are finite; a program needn't handle non-finite values.
Results may differ from a plain program's by a relative error of at most 0.017.
Values may be sent and summed in bfloat16 or wider, within the bound.
No kernel may reach another device: no remote copies, remote signals or barrier semaphores. Data moves between devices by JAX's collectives and lax.ppermute only.
A program may use at most 128 MiB of HBM per device.

v0:
```python
import jax
import jax.numpy as jnp
from jax import lax
from jax.experimental import pallas as pl
from jax.experimental.pallas import tpu as pltpu
from jax.sharding import PartitionSpec as P

CAP_PAIR = 20
PAD_PAIR = 24
ROW_TILE = 160
FOLD_TILE = 32


def move(x, by):
    return lax.ppermute(x, "rep", [(i, (i + 2 * by) % 8) for i in range(8)])


def swap(x):
    return lax.ppermute(x, "rep", [(i, i ^ 1) for i in range(8)])


def place_rows(slot_ids, n_ep):
    flat = slot_ids.T.reshape(-1)
    count = flat.shape[0]
    onehot = (flat[:, None] == jnp.arange(2 * n_ep, dtype=jnp.int32)[None, :]).astype(jnp.bfloat16)
    before = jnp.tril(jnp.ones((count, count), jnp.bfloat16), -1)
    ahead = jnp.dot(before, onehot, preferred_element_type=jnp.float32)
    position = jnp.sum(ahead * onehot.astype(jnp.float32), axis=1).astype(jnp.int32)
    odd = flat % 2
    expert = (flat // 2 - odd + n_ep) % n_ep
    row = expert * PAD_PAIR + odd * (CAP_PAIR // 2) + position
    return row.reshape(2, -1)


def exchange(rows, n_ep):
    width = rows.shape[1]
    out = lax.all_to_all(rows.reshape(n_ep, PAD_PAIR, width), "ep", 0, 0, tiled=True)
    return out.reshape(n_ep * PAD_PAIR, width)


def compact_matrix(pairs):
    r = lax.broadcasted_iota(jnp.int32, (pairs * CAP_PAIR, pairs * PAD_PAIR), 0)
    c = lax.broadcasted_iota(jnp.int32, (pairs * CAP_PAIR, pairs * PAD_PAIR), 1)
    return (r // CAP_PAIR * PAD_PAIR + r % CAP_PAIR == c).astype(jnp.bfloat16)


def pick(matrix, rows):
    return jnp.dot(matrix, rows, preferred_element_type=jnp.float32).astype(jnp.bfloat16)


def after(value, *first):
    return lax.optimization_barrier((value, *first))[0]


class Order:
    def __init__(self):
        self.last = ()

    def __call__(self, *values):
        out = lax.optimization_barrier((*values, *self.last))[: len(values)]
        self.last = out
        return out if len(out) > 1 else out[0]


def mm(a, b):
    return jnp.dot(a, b, preferred_element_type=jnp.float32)


def add(*terms):
    return sum(t.astype(jnp.float32) for t in terms).astype(jnp.bfloat16)


def halves(x):
    half = x.shape[0] // 2
    return x[:half], x[half:]


def block(idx, i, width):
    return pl.ds(pl.multiple_of(idx[i] * width, width), width)


def first_kernel(idx, *refs):
    xs, (wg, wu, *outs) = refs[:8], refs[8:]
    rows, width = xs[0].shape

    @pl.loop(0, rows // ROW_TILE)
    def _(i):
        at = pl.ds(pl.multiple_of(i * ROW_TILE, ROW_TILE), ROW_TILE)
        for p in range(2):
            for m, w in enumerate((wg, wu)):
                outs[2 * p + m][at, :] = sum(
                    mm(xs[2 * n + p][at, :], w[block(idx, d, width), :])
                    for n, d in enumerate((0, 1, 3, 2))
                )


def second_kernel(idx, g_in, u_in, *refs):
    xs, (wg, wu, wd, h_ref, top, bottom, *sums) = refs[:5], refs[5:]
    half, width = top.shape

    @pl.loop(0, 2)
    def _(i):
        at = pl.ds(pl.multiple_of(i * half, half), half)
        for w, start, total in zip((wg, wu), (g_in, u_in), sums):
            total[at, :] = start[at, :] + sum(
                mm(x[at, :], w[block(idx, d, width), :]) for x, d in zip(xs[:3], (4, 5, 7))
            )

    for h, (x, out) in enumerate(zip(xs[3:], (top, bottom))):
        at = slice(h * half, (h + 1) * half)
        gate, up = [
            total[at, :] + mm(x[...], w[block(idx, 6, width), :])
            for w, total in zip((wg, wu), sums)
        ]
        hidden = (gate / (1.0 + jnp.exp(-gate)) * up).astype(jnp.bfloat16)
        h_ref[at, :] = hidden
        out[...] = mm(hidden, wd[:, block(idx, 6, width)]).astype(jnp.bfloat16)


REST = (5, 7, 4, 2, 1, 3, 0)


def third_kernel(idx, h_ref, wd, *outs):
    rows, width = outs[0].shape

    @pl.loop(0, rows // ROW_TILE)
    def _(j):
        at = pl.ds(pl.multiple_of(j * ROW_TILE, ROW_TILE), ROW_TILE)
        hidden = h_ref[at, :]
        for i, out in zip(REST, outs):
            out[at, :] = mm(hidden, wd[:, block(idx, i, width)]).astype(jnp.bfloat16)


def fold_kernel(one, three, top, bottom, one_out, three_out):
    half = top.shape[0]

    @pl.loop(0, half // FOLD_TILE)
    def _(i):
        upper = pl.ds(pl.multiple_of(i * FOLD_TILE, FOLD_TILE), FOLD_TILE)
        lower = pl.ds(pl.multiple_of(half + i * FOLD_TILE, FOLD_TILE), FOLD_TILE)
        one_out[upper, :] = add(one[upper, :], top[upper, :])
        one_out[lower, :] = one[lower, :]
        three_out[upper, :] = three[upper, :]
        three_out[lower, :] = add(three[lower, :], bottom[upper, :])


def call(body, outs, flops, *args, scratch=()):
    smem = pl.BlockSpec(memory_space=pltpu.SMEM)
    vmem = pl.BlockSpec(memory_space=pltpu.VMEM)
    size = sum(a.size * a.dtype.itemsize for a in (*args, *outs))
    return pl.pallas_call(
        body,
        in_specs=[smem if a.ndim == 1 else vmem for a in args],
        out_specs=[vmem] * len(outs),
        out_shape=outs,
        scratch_shapes=scratch,
        compiler_params=pltpu.CompilerParams(vmem_limit_bytes=16 * 2**20),
        cost_estimate=pl.CostEstimate(flops=flops, bytes_accessed=size, transcendentals=0),
    )(*args)


def bf16(*shape):
    return jax.ShapeDtypeStruct(shape, jnp.bfloat16)


def fold(*terms):
    return call(fold_kernel, [bf16(*terms[0].shape)] * 2, terms[0].size, *terms)


def near(x):
    return move(x, 1), move(x, -1)


def far(left, right):
    return move(halves(left)[0], 1), move(halves(right)[1], -1)


def shards(tokens, slot_ids, weights, w_gate, w_up, w_down):
    n_ep = lax.axis_size("ep")
    rep = lax.axis_index("rep")
    around = [(rep + 2 * d) & 7 for d in range(4)]
    idx = jnp.stack(around + [a ^ 1 for a in around]).astype(jnp.int32)
    w_gate, w_up, w_down = w_gate[0], w_up[0], w_down[0]

    row = place_rows(slot_ids, n_ep)
    slots = lax.broadcasted_iota(jnp.int32, (n_ep * PAD_PAIR, tokens.shape[0]), 0)
    pack = ((slots == row[0][None]) | (slots == row[1][None])).astype(jnp.bfloat16)
    compact = compact_matrix(n_ep // 2)
    middle = n_ep * PAD_PAIR // 2

    arrived = exchange(pick(pack, tokens), n_ep)
    top, bottom = pick(compact, arrived[:middle]), pick(compact, arrived[middle:])
    width, hidden = tokens.shape[1], w_gate.shape[1]
    order = Order()

    def units(sums, *xs):
        rows = xs[0].shape[0]
        return call(
            second_kernel,
            [bf16(rows, hidden), bf16(rows // 2, width), bf16(rows // 2, width)],
            18 * rows * width * hidden,
            idx,
            *sums,
            *xs,
            w_gate,
            w_up,
            w_down,
            scratch=[pltpu.VMEM((rows, hidden), jnp.float32)] * 2,
        )

    def terms(hid):
        rows = hid.shape[0]
        return call(
            third_kernel,
            [bf16(rows, width)] * len(REST),
            14 * rows * width * hidden,
            idx,
            hid,
            w_down,
        )

    lt, rb = move(top, 1), move(bottom, -1)
    swap1 = swap(top)
    ft, fb = move(lt, 1), move(rb, -1)
    swap2 = swap(after(bottom, lt, rb))
    lb, rt = move(after(bottom, rb), 1), move(after(top, lt), -1)
    acc = lambda x: [jax.ShapeDtypeStruct((x.shape[0], hidden), jnp.float32)] * 2
    sums = call(
        first_kernel,
        acc(top) + acc(bottom),
        32 * top.shape[0] * width * hidden,
        idx,
        *(top, bottom, rt, rb, lt, lb, ft, fb),
        w_gate,
        w_up,
    )
    o1 = after(swap1, lb, rt)
    l1, r1 = near(o1)
    f1a, f1b = far(l1, r1)
    o2 = after(swap2, *sums, l1, r1)
    l2, r2 = near(o2)
    f1a, f1b = order(f1a, f1b)

    hid, ga, gb = order(*units(sums[:2], o1, r1, l1, f1a, f1b))
    ga, gb = move(ga, 1), move(gb, -1)
    t5, t7, t4, t2, t1, t3, t0 = terms(hid)
    l2, r2 = order(l2, r2)
    f2a, f2b = far(l2, r2)
    ga, gb = order(ga, gb)
    one, three = fold(t5, t7, ga, gb)
    ol, orr = move(one, 1), move(three, -1)
    f2a, f2b = order(f2a, f2b)
    hid, ga, gb = order(*units(sums[2:], o2, r2, l2, f2a, f2b))
    ga, gb = move(ga, 1), move(gb, -1)
    b5, b7, b4, b2, b1, b3, b0 = terms(hid)
    ol, orr = order(ol, orr)
    came1 = swap(add(t4, ol, orr))
    ga, gb = order(ga, gb)
    one, three = fold(b5, b7, ga, gb)
    ol, orr = move(one, 1), move(three, -1)

    ft, fb = move(lax.optimization_barrier((t2, ga))[0], 1), move(b2, -1)
    ol, orr = order(ol, orr)
    came2 = swap(add(b4, ol, orr))
    lb = move(lax.optimization_barrier((b1, ol))[0], 1)
    rt = move(lax.optimization_barrier((t3, orr))[0], -1)
    came1 = order(came1)
    ft, fb = order(ft, fb)
    lt, rb = move(add(t1, ft), 1), move(add(b3, fb), -1)
    lb, rt = order(lb, rt)
    lt, rb = order(lt, rb)
    spread = compact.T
    total = [pick(spread, add(t0, lt, rt, came1)), pick(spread, add(b0, lb, rb, came2))]
    back = exchange(jnp.concatenate(total, axis=0), n_ep)

    columns = lax.broadcasted_iota(jnp.int32, (tokens.shape[0], n_ep * PAD_PAIR), 1)
    out = sum(
        weights[:, k : k + 1] * mm((columns == row[k][:, None]).astype(jnp.bfloat16), back)
        for k in range(2)
    )
    return out.astype(jnp.bfloat16)


def solution(mesh):
    placed = (
        P("ep", "rep"),
        P("ep", None),
        P("ep", None),
        P("ep", None, "rep"),
        P("ep", None, "rep"),
        P("ep", "rep", None),
    )
    return jax.shard_map(
        shards, mesh=mesh, in_specs=placed, out_specs=P("ep", "rep"), check_vma=False
    )
```

profile of v0, /device:TPU:1, one launch (start us, length us, event | category | flops | bytes accessed | tf_op | source)
XLA Modules:
  0.0 263.4 jit_solution(965373980159577935)
XLA Ops:
  1.2 1.7 convolution_convert_fusion
  2.9 10.2 %all-to-all-start = ((bf16[32,24,896]{2,1,0:T(8,128)(2,1)}), bf16[32,24,896]{2,1,0:T(8,128)(2,1)S(1)}, u32[]{:S(2)}, u32[]{:S(2)}) async-start(bf16[32,24,896]{2,1,0:T(8,128)(2,1)} %bitcast.10), calls=%async_computation | async-start | bytes 2752512 | tf_op jit(solution)/shard_map/all_to_all | solution.py:37
  13.1 34.7 %all-to-all-done = bf16[32,24,896]{2,1,0:T(8,128)(2,1)S(1)} async-done(((bf16[32,24,896]{2,1,0:T(8,128)(2,1)}), bf16[32,24,896]{2,1,0:T(8,128)(2,1)S(1)}, u32[]{:S(2)}, u32[]{:S(2)}) %all-to-all-start) | async-done | bytes 1376288 | tf_op jit(solution)/shard_map/all_to_all | solution.py:37
  48.7 2.6 collective-permute-start.2
  52.1 4.3 %collective-permute-start.6 = (bf16[320,896]{1,0:T(8,128)(2,1)S(1)}, bf16[320,896]{1,0:T(8,128)(2,1)S(1)}, u32[]{:S(2)}, u32[]{:S(2)}) collective-permute-start(bf16[320,896]{1,0:T(8,128)(2,1)S(1)} %convolution_convert_fusion.4.refs_0_), channel_id=1, source_target_pairs={{0,32},{32,0},{64,96},{96,64},{128,160},{160,128},{192,224},{224,1... | collective-permute-start | bytes 1720328 | tf_op jit(solution)/shard_map/ppermute | solution.py:19
  56.4 6.8 %collective-permute-done.2.refs_3_ = bf16[320,896]{1,0:T(8,128)(2,1)} collective-permute-done((bf16[320,896]{1,0:T(8,128)(2,1)S(1)}, bf16[320,896]{1,0:T(8,128)(2,1)}, u32[]{:S(2)}, u32[]{:S(2)}) %collective-permute-start.2) | collective-permute-done | bytes 573472 | tf_op jit(solution)/shard_map/ppermute | solution.py:15
  64.2 3.0 %collective-permute-done.refs_4_ = bf16[320,896]{1,0:T(8,128)(2,1)} collective-permute-done((bf16[320,896]{1,0:T(8,128)(2,1)S(1)}, bf16[320,896]{1,0:T(8,128)(2,1)}, u32[]{:S(2)}, u32[]{:S(2)}) %collective-permute-start) | collective-permute-done | bytes 573472 | tf_op jit(solution)/shard_map/ppermute | solution.py:15
  69.5 13.1 %collective-permute-done.6.refs_0_ = bf16[320,896]{1,0:T(8,128)(2,1)S(1)} collective-permute-done((bf16[320,896]{1,0:T(8,128)(2,1)S(1)}, bf16[320,896]{1,0:T(8,128)(2,1)S(1)}, u32[]{:S(2)}, u32[]{:S(2)}) %collective-permute-start.6) | collective-permute-done | bytes 573472 | tf_op jit(solution)/shard_map/ppermute | solution.py:19
  84.2 2.5 collective-permute-start.7
  86.8 2.2 collective-permute-start.11
  89.0 3.2 %collective-permute-done.5.refs_7_ = bf16[320,896]{1,0:T(8,128)(2,1)} collective-permute-done((bf16[320,896]{1,0:T(8,128)(2,1)}, bf16[320,896]{1,0:T(8,128)(2,1)}, u32[]{:S(2)}, u32[]{:S(2)}) %collective-permute-start.5) | collective-permute-done | bytes 573472 | tf_op jit(solution)/shard_map/ppermute | solution.py:15
  92.2 2.0 copy-done.2
  94.3 2.0 copy-done.4
  99.5 4.8 %shard_map.64 = (f32[320,256]{1,0:T(8,128)S(1)}, f32[320,256]{1,0:T(8,128)S(1)}, f32[320,256]{1,0:T(8,128)S(1)}, f32[320,256]{1,0:T(8,128)S(1)}) custom-call(s32[8]{0:T(128)S(1)} %stack.35.idx, bf16[320,896]{1,0:T(8,128)(2,1)S(1)} %copy-done.7, bf16[320,896]{1,0:T(8,128)(2,1)S(1)} %convolution_convert_fusion.3.refs_1_, bf16[320,896]{1,0:T(8,128)(2,1)S(1)} %copy-done.11, ...), custom_call_target="tpu_custom_call" | custom-call | flops 2348810240 | bytes 13238304 | tf_op jit(solution)/shard_map/pallas_call | solution.py:151
  104.4 1.8 collective-permute-start.10
  106.3 10.4 %collective-permute-done.11.refs_0_ = bf16[320,896]{1,0:T(8,128)(2,1)S(1)} collective-permute-done((bf16[320,896]{1,0:T(8,128)(2,1)S(1)}, bf16[320,896]{1,0:T(8,128)(2,1)S(1)}, u32[]{:S(2)}, u32[]{:S(2)}) %collective-permute-start.11) | collective-permute-done | bytes 573472 | tf_op jit(solution)/shard_map/ppermute | solution.py:19
  116.7 2.7 %collective-permute-start.13 = (bf16[320,896]{1,0:T(8,128)(2,1)S(1)}, bf16[320,896]{1,0:T(8,128)(2,1)S(1)}, u32[]{:S(2)}, u32[]{:S(2)}) collective-permute-start(bf16[320,896]{1,0:T(8,128)(2,1)S(1)} %collective-permute-done.11.refs_0_), channel_id=1, source_target_pairs={{0,192},{32,224},{64,0},{96,32},{128,64},{160,96},{192,128},{224,1... | collective-permute-start | bytes 1720328 | tf_op jit(solution)/shard_map/ppermute | solution.py:15
  119.4 2.9 %shard_map.65 = (bf16[320,256]{1,0:T(8,128)(2,1)S(1)}, bf16[160,896]{1,0:T(8,128)(2,1)S(1)}, bf16[160,896]{1,0:T(8,128)(2,1)S(1)}) custom-call(s32[8]{0:T(128)S(1)} %stack.35.idx, f32[320,256]{1,0:T(8,128)S(1)} %get-tuple-element.70.g_in, f32[320,256]{1,0:T(8,128)S(1)} %get-tuple-element.71.u_in, bf16[320,896]{1,0:T(8,128)(2,1)S(1)} %collective-permute-done.6.refs_0_, ...), custom_call_target="tpu_custom_call" | custom-call | flops 1321205760 | bytes 14696480 | tf_op jit(solution)/shard_map/pallas_call | solution.py:151
  122.4 2.7 %collective-permute-start.17 = (bf16[160,896]{1,0:T(8,128)(2,1)S(1)}, bf16[160,896]{1,0:T(8,128)(2,1)S(1)}, u32[]{:S(2)}, u32[]{:S(2)}) collective-permute-start(bf16[160,896]{1,0:T(8,128)(2,1)S(1)} %get-tuple-element.87), channel_id=1, source_target_pairs={{0,192},{32,224},{64,0},{96,32},{128,64},{160,96},{192,128},{224,1... | collective-permute-start | bytes 860168 | tf_op jit(solution)/shard_map/ppermute | solution.py:15
  125.0 6.9 %collective-permute-done.12.refs_2_ = bf16[320,896]{1,0:T(8,128)(2,1)S(1)} collective-permute-done((bf16[320,896]{1,0:T(8,128)(2,1)S(1)}, bf16[320,896]{1,0:T(8,128)(2,1)S(1)}, u32[]{:S(2)}, u32[]{:S(2)}) %collective-permute-start.12) | collective-permute-done | bytes 573472 | tf_op jit(solution)/shard_map/ppermute | solution.py:15
  132.9 1.9 collective-permute-start.15
  134.8 2.1 shard_map.66
  137.0 1.1 collective-permute-done.16.top
  139.2 1.9 collective-permute-start.21
  141.0 3.2 %collective-permute-done.14.refs_3_ = bf16[160,896]{1,0:T(8,128)(2,1)S(1)} collective-permute-done((bf16[160,896]{1,0:T(8,128)(2,1)S(1)}, bf16[160,896]{1,0:T(8,128)(2,1)S(1)}, u32[]{:S(2)}, u32[]{:S(2)}) %collective-permute-start.14) | collective-permute-done | bytes 286752 | tf_op jit(solution)/shard_map/ppermute | solution.py:15
  144.2 2.9 %shard_map.67 = (bf16[320,256]{1,0:T(8,128)(2,1)S(1)}, bf16[160,896]{1,0:T(8,128)(2,1)S(1)}, bf16[160,896]{1,0:T(8,128)(2,1)S(1)}) custom-call(s32[8]{0:T(128)S(1)} %stack.35.idx, f32[320,256]{1,0:T(8,128)S(1)} %get-tuple-element.82.g_in, f32[320,256]{1,0:T(8,128)S(1)} %get-tuple-element.83.u_in, bf16[320,896]{1,0:T(8,128)(2,1)S(1)} %collective-permute-done.11.refs_0_, ...), custom_call_target="tpu_custom_call" | custom-call | flops 1321205760 | bytes 14696480 | tf_op jit(solution)/shard_map/pallas_call | solution.py:151
  148.0 1.9 collective-permute-start.19
  149.9 2.1 shard_map.69
  152.0 1.4 collective-permute-start.23
  153.4 3.1 %collective-permute-done.20 = bf16[320,896]{1,0:T(8,128)(2,1)S(1)} collective-permute-done((bf16[320,896]{1,0:T(8,128)(2,1)S(1)}, bf16[320,896]{1,0:T(8,128)(2,1)S(1)}, u32[]{:S(2)}, u32[]{:S(2)}) %collective-permute-start.20) | collective-permute-done | bytes 573472 | tf_op jit(solution)/shard_map/ppermute | solution.py:15
  156.5 6.1 %collective-permute-done.18.top = bf16[160,896]{1,0:T(8,128)(2,1)S(1)} collective-permute-done((bf16[160,896]{1,0:T(8,128)(2,1)S(1)}, bf16[160,896]{1,0:T(8,128)(2,1)S(1)}, u32[]{:S(2)}, u32[]{:S(2)}) %collective-permute-start.18) | collective-permute-done | bytes 286752 | tf_op jit(solution)/shard_map/ppermute | solution.py:15
  163.8 1.9 collective-permute-start.26
  165.8 2.3 collective-permute-start.24
  168.1 8.2 %collective-permute-done.25 = bf16[320,896]{1,0:T(8,128)(2,1)S(1)} collective-permute-done((bf16[320,896]{1,0:T(8,128)(2,1)S(1)}, bf16[320,896]{1,0:T(8,128)(2,1)S(1)}, u32[]{:S(2)}, u32[]{:S(2)}) %collective-permute-start.25) | collective-permute-done | bytes 573472 | tf_op jit(solution)/shard_map/ppermute | solution.py:15
  176.3 9.9 %collective-permute-done.26 = bf16[320,896]{1,0:T(8,128)(2,1)S(1)} collective-permute-done((bf16[320,896]{1,0:T(8,128)(2,1)S(1)}, bf16[320,896]{1,0:T(8,128)(2,1)S(1)}, u32[]{:S(2)}, u32[]{:S(2)}) %collective-permute-start.26) | collective-permute-done | bytes 573472 | tf_op jit(solution)/shard_map/ppermute | solution.py:15
  186.2 3.4 %collective-permute-start.30 = (bf16[320,896]{1,0:T(8,128)(2,1)S(1)}, bf16[320,896]{1,0:T(8,128)(2,1)S(1)}, u32[]{:S(2)}, u32[]{:S(2)}) collective-permute-start(bf16[320,896]{1,0:T(8,128)(2,1)S(1)} %get-tuple-element.124), channel_id=1, source_target_pairs={{0,192},{32,224},{64,0},{96,32},{128,64},{160,96},{192,128},{224,1... | collective-permute-start | bytes 1720328 | tf_op jit(solution)/shard_map/ppermute | solution.py:15
  189.6 5.3 %collective-permute-done.24 = bf16[320,896]{1,0:T(8,128)(2,1)S(1)} collective-permute-done((bf16[320,896]{1,0:T(8,128)(2,1)S(1)}, bf16[320,896]{1,0:T(8,128)(2,1)S(1)}, u32[]{:S(2)}, u32[]{:S(2)}) %collective-permute-start.24) | collective-permute-done | bytes 573472 | tf_op jit(solution)/shard_map/ppermute | solution.py:19
  195.3 1.5 collective-permute-start.27
  197.1 1.3 collective-permute-start.31
  198.4 1.8 collective-permute-done.30
  200.2 3.1 %collective-permute-done.29 = bf16[320,896]{1,0:T(8,128)(2,1)S(1)} collective-permute-done((bf16[320,896]{1,0:T(8,128)(2,1)S(1)}, bf16[320,896]{1,0:T(8,128)(2,1)S(1)}, u32[]{:S(2)}, u32[]{:S(2)}) %collective-permute-start.29) | collective-permute-done | bytes 573472 | tf_op jit(solution)/shard_map/ppermute | solution.py:15
  203.3 9.2 %collective-permute-done.28 = bf16[320,896]{1,0:T(8,128)(2,1)S(1)} collective-permute-done((bf16[320,896]{1,0:T(8,128)(2,1)S(1)}, bf16[320,896]{1,0:T(8,128)(2,1)S(1)}, u32[]{:S(2)}, u32[]{:S(2)}) %collective-permute-start.28) | collective-permute-done | bytes 573472 | tf_op jit(solution)/shard_map/ppermute | solution.py:15
  212.5 3.1 %collective-permute-done.27 = bf16[320,896]{1,0:T(8,128)(2,1)S(1)} collective-permute-done((bf16[320,896]{1,0:T(8,128)(2,1)S(1)}, bf16[320,896]{1,0:T(8,128)(2,1)S(1)}, u32[]{:S(2)}, u32[]{:S(2)}) %collective-permute-start.27) | collective-permute-done | bytes 573472 | tf_op jit(solution)/shard_map/ppermute | solution.py:15
  216.6 3.8 %collective-permute-done.31 = bf16[320,896]{1,0:T(8,128)(2,1)S(1)} collective-permute-done((bf16[320,896]{1,0:T(8,128)(2,1)S(1)}, bf16[320,896]{1,0:T(8,128)(2,1)S(1)}, u32[]{:S(2)}, u32[]{:S(2)}) %collective-permute-start.31) | collective-permute-done | bytes 573472 | tf_op jit(solution)/shard_map/ppermute | solution.py:19
  221.4 1.2 pad_maximum_fusion
  222.6 4.2 %all-to-all-start.1 = ((bf16[32,24,896]{2,1,0:T(8,128)(2,1)}), bf16[32,24,896]{2,1,0:T(8,128)(2,1)S(1)}, u32[]{:S(2)}, u32[]{:S(2)}) async-start(bf16[32,24,896]{2,1,0:T(8,128)(2,1)} %bitcast.16), calls=%async_computation.1 | async-start | bytes 2752512 | tf_op jit(solution)/shard_map/all_to_all | solution.py:37
  226.9 34.9 %all-to-all-done.1 = bf16[32,24,896]{2,1,0:T(8,128)(2,1)S(1)} async-done(((bf16[32,24,896]{2,1,0:T(8,128)(2,1)}), bf16[32,24,896]{2,1,0:T(8,128)(2,1)S(1)}, u32[]{:S(2)}, u32[]{:S(2)}) %all-to-all-start.1) | async-done | bytes 1376288 | tf_op jit(solution)/shard_map/all_to_all | solution.py:37
  262.2 1.2 fusion.1
  (80 shorter events, 18.6 us)
Async XLA Ops:
  0.0 1.2 copy-start
  2.9 45.0 %all-to-all-start = ((bf16[32,24,896]{2,1,0:T(8,128)(2,1)}), bf16[32,24,896]{2,1,0:T(8,128)(2,1)S(1)}, u32[]{:S(2)}, u32[]{:S(2)}) async-start(bf16[32,24,896]{2,1,0:T(8,128)(2,1)} %bitcast.10), calls=%async_computation | async-start | bytes 2752512 | tf_op jit(solution)/shard_map/all_to_all | solution.py:37
  48.7 14.5 %collective-permute-start.2 = (bf16[320,896]{1,0:T(8,128)(2,1)S(1)}, bf16[320,896]{1,0:T(8,128)(2,1)}, u32[]{:S(2)}, u32[]{:S(2)}) collective-permute-start(bf16[320,896]{1,0:T(8,128)(2,1)S(1)} %convolution_convert_fusion.3.refs_1_), channel_id=1, source_target_pairs={{0,192},{32,224},{64,0},{96,32},{128,64},{160,96},{192,128},{224,1... | collective-permute-start | bytes 1720328 | tf_op jit(solution)/shard_map/ppermute | solution.py:15
  52.0 15.2 %collective-permute-start = (bf16[320,896]{1,0:T(8,128)(2,1)S(1)}, bf16[320,896]{1,0:T(8,128)(2,1)}, u32[]{:S(2)}, u32[]{:S(2)}) collective-permute-start(bf16[320,896]{1,0:T(8,128)(2,1)S(1)} %convolution_convert_fusion.4.refs_0_), channel_id=1, source_target_pairs={{0,64},{32,96},{64,128},{96,160},{128,192},{160,224},{192,0},{224,... | collective-permute-start | bytes 1720328 | tf_op jit(solution)/shard_map/ppermute | solution.py:15
  52.1 30.5 %collective-permute-start.6 = (bf16[320,896]{1,0:T(8,128)(2,1)S(1)}, bf16[320,896]{1,0:T(8,128)(2,1)S(1)}, u32[]{:S(2)}, u32[]{:S(2)}) collective-permute-start(bf16[320,896]{1,0:T(8,128)(2,1)S(1)} %convolution_convert_fusion.4.refs_0_), channel_id=1, source_target_pairs={{0,32},{32,0},{64,96},{96,64},{128,160},{160,128},{192,224},{224,1... | collective-permute-start | bytes 1720328 | tf_op jit(solution)/shard_map/ppermute | solution.py:19
  63.2 19.4 %collective-permute-start.3 = (bf16[320,896]{1,0:T(8,128)(2,1)S(1)}, bf16[320,896]{1,0:T(8,128)(2,1)S(1)}, u32[]{:S(2)}, u32[]{:S(2)}) collective-permute-start(bf16[320,896]{1,0:T(8,128)(2,1)S(1)} %convolution_convert_fusion.3.refs_1_), channel_id=1, source_target_pairs={{0,64},{32,96},{64,128},{96,160},{128,192},{160,224},{192,0},{224,... | collective-permute-start | bytes 1720328 | tf_op jit(solution)/shard_map/ppermute | solution.py:15
  67.2 16.2 %collective-permute-start.1 = (bf16[320,896]{1,0:T(8,128)(2,1)S(1)}, bf16[320,896]{1,0:T(8,128)(2,1)S(1)}, u32[]{:S(2)}, u32[]{:S(2)}) collective-permute-start(bf16[320,896]{1,0:T(8,128)(2,1)S(1)} %convolution_convert_fusion.4.refs_0_), channel_id=1, source_target_pairs={{0,192},{32,224},{64,0},{96,32},{128,64},{160,96},{192,128},{224,1... | collective-permute-start | bytes 1720328 | tf_op jit(solution)/shard_map/ppermute | solution.py:15
  67.2 0.8 copy-start.6
  68.1 24.2 %collective-permute-start.5 = (bf16[320,896]{1,0:T(8,128)(2,1)}, bf16[320,896]{1,0:T(8,128)(2,1)}, u32[]{:S(2)}, u32[]{:S(2)}) collective-permute-start(bf16[320,896]{1,0:T(8,128)(2,1)} %collective-permute-done.2.refs_3_), channel_id=1, source_target_pairs={{0,192},{32,224},{64,0},{96,32},{128,64},{160,96},{192,128},{224,1... | collective-permute-start | bytes 1720328 | tf_op jit(solution)/shard_map/ppermute | solution.py:15
  69.0 23.2 %collective-permute-start.4 = (bf16[320,896]{1,0:T(8,128)(2,1)}, bf16[320,896]{1,0:T(8,128)(2,1)}, u32[]{:S(2)}, u32[]{:S(2)}) collective-permute-start(bf16[320,896]{1,0:T(8,128)(2,1)} %collective-permute-done.refs_4_), channel_id=1, source_target_pairs={{0,64},{32,96},{64,128},{96,160},{128,192},{160,224},{192,0},{224,... | collective-permute-start | bytes 1720328 | tf_op jit(solution)/shard_map/ppermute | solution.py:15
  82.6 0.8 copy-start.8
  83.4 0.8 copy-start.10
  84.2 20.2 %collective-permute-start.7 = (bf16[320,896]{1,0:T(8,128)(2,1)S(1)}, bf16[320,896]{1,0:T(8,128)(2,1)S(1)}, u32[]{:S(2)}, u32[]{:S(2)}) collective-permute-start(bf16[320,896]{1,0:T(8,128)(2,1)S(1)} %collective-permute-done.6.refs_0_), channel_id=1, source_target_pairs={{0,192},{32,224},{64,0},{96,32},{128,64},{160,96},{192,128},{224,1... | collective-permute-start | bytes 1720328 | tf_op jit(solution)/shard_map/ppermute | solution.py:15
  86.8 19.4 %collective-permute-start.8 = (bf16[320,896]{1,0:T(8,128)(2,1)S(1)}, bf16[320,896]{1,0:T(8,128)(2,1)S(1)}, u32[]{:S(2)}, u32[]{:S(2)}) collective-permute-start(bf16[320,896]{1,0:T(8,128)(2,1)S(1)} %collective-permute-done.6.refs_0_), channel_id=1, source_target_pairs={{0,64},{32,96},{64,128},{96,160},{128,192},{160,224},{192,0},{224,... | collective-permute-start | bytes 1720328 | tf_op jit(solution)/shard_map/ppermute | solution.py:15
  86.8 29.9 %collective-permute-start.11 = (bf16[320,896]{1,0:T(8,128)(2,1)S(1)}, bf16[320,896]{1,0:T(8,128)(2,1)S(1)}, u32[]{:S(2)}, u32[]{:S(2)}) collective-permute-start(bf16[320,896]{1,0:T(8,128)(2,1)S(1)} %convolution_convert_fusion.3.refs_1_), channel_id=1, source_target_pairs={{0,32},{32,0},{64,96},{96,64},{128,160},{160,128},{192,224},{224,1... | collective-permute-start | bytes 1720328 | tf_op jit(solution)/shard_map/ppermute | solution.py:19
  92.2 2.0 copy-start.2
  94.3 2.0 copy-start.4
  96.3 1.1 copy-start.7
  97.4 1.1 copy-start.9
  98.4 1.1 copy-start.11
  99.5 19.9 %copy-start.1 = (bf16[1,256,7168]{2,1,0:T(8,128)(2,1)S(1)}, bf16[1,256,7168]{2,1,0:T(8,128)(2,1)}, u32[]{:S(2)}) copy-start(bf16[1,256,7168]{2,1,0:T(8,128)(2,1)} %param.11) | copy-start | bytes 11010052
  99.5 19.9 %copy-start.3 = (bf16[1,7168,256]{2,1,0:T(8,128)(2,1)S(1)}, bf16[1,7168,256]{2,1,0:T(8,128)(2,1)}, u32[]{:S(2)}) copy-start(bf16[1,7168,256]{2,1,0:T(8,128)(2,1)} %param.9) | copy-start | bytes 11010052
  99.5 19.9 %copy-start.5 = (bf16[1,7168,256]{2,1,0:T(8,128)(2,1)S(1)}, bf16[1,7168,256]{2,1,0:T(8,128)(2,1)}, u32[]{:S(2)}) copy-start(bf16[1,7168,256]{2,1,0:T(8,128)(2,1)} %param.10) | copy-start | bytes 11010052
  104.4 14.9 %collective-permute-start.10 = (bf16[160,896]{1,0:T(8,128)(2,1)S(1)}, bf16[160,896]{1,0:T(8,128)(2,1)S(1)}, u32[]{:S(2)}, u32[]{:S(2)}) collective-permute-start(bf16[160,896]{1,0:T(8,128)(2,1)S(1)} %slice.55), channel_id=1, source_target_pairs={{0,192},{32,224},{64,0},{96,32},{128,64},{160,96},{192,128},{224,1... | collective-permute-start | bytes 860168 | tf_op jit(solution)/shard_map/ppermute | solution.py:15
  106.2 13.2 %collective-permute-start.9 = (bf16[160,896]{1,0:T(8,128)(2,1)S(1)}, bf16[160,896]{1,0:T(8,128)(2,1)S(1)}, u32[]{:S(2)}, u32[]{:S(2)}) collective-permute-start(bf16[160,896]{1,0:T(8,128)(2,1)S(1)} %slice.54), channel_id=1, source_target_pairs={{0,64},{32,96},{64,128},{96,160},{128,192},{160,224},{192,0},{224,... | collective-permute-start | bytes 860168 | tf_op jit(solution)/shard_map/ppermute | solution.py:15
  116.7 15.3 %collective-permute-start.12 = (bf16[320,896]{1,0:T(8,128)(2,1)S(1)}, bf16[320,896]{1,0:T(8,128)(2,1)S(1)}, u32[]{:S(2)}, u32[]{:S(2)}) collective-permute-start(bf16[320,896]{1,0:T(8,128)(2,1)S(1)} %collective-permute-done.11.refs_0_), channel_id=1, source_target_pairs={{0,64},{32,96},{64,128},{96,160},{128,192},{160,224},{192,0},{224,... | collective-permute-start | bytes 1720328 | tf_op jit(solution)/shard_map/ppermute | solution.py:15
  116.7 15.3 %collective-permute-start.13 = (bf16[320,896]{1,0:T(8,128)(2,1)S(1)}, bf16[320,896]{1,0:T(8,128)(2,1)S(1)}, u32[]{:S(2)}, u32[]{:S(2)}) collective-permute-start(bf16[320,896]{1,0:T(8,128)(2,1)S(1)} %collective-permute-done.11.refs_0_), channel_id=1, source_target_pairs={{0,192},{32,224},{64,0},{96,32},{128,64},{160,96},{192,128},{224,1... | collective-permute-start | bytes 1720328 | tf_op jit(solution)/shard_map/ppermute | solution.py:15
  122.3 15.8 %collective-permute-start.16 = (bf16[160,896]{1,0:T(8,128)(2,1)S(1)}, bf16[160,896]{1,0:T(8,128)(2,1)S(1)}, u32[]{:S(2)}, u32[]{:S(2)}) collective-permute-start(bf16[160,896]{1,0:T(8,128)(2,1)S(1)} %get-tuple-element.86), channel_id=1, source_target_pairs={{0,64},{32,96},{64,128},{96,160},{128,192},{160,224},{192,0},{224,... | collective-permute-start | bytes 860168 | tf_op jit(solution)/shard_map/ppermute | solution.py:15
  122.4 15.7 %collective-permute-start.17 = (bf16[160,896]{1,0:T(8,128)(2,1)S(1)}, bf16[160,896]{1,0:T(8,128)(2,1)S(1)}, u32[]{:S(2)}, u32[]{:S(2)}) collective-permute-start(bf16[160,896]{1,0:T(8,128)(2,1)S(1)} %get-tuple-element.87), channel_id=1, source_target_pairs={{0,192},{32,224},{64,0},{96,32},{128,64},{160,96},{192,128},{224,1... | collective-permute-start | bytes 860168 | tf_op jit(solution)/shard_map/ppermute | solution.py:15
  132.0 12.3 %collective-permute-start.14 = (bf16[160,896]{1,0:T(8,128)(2,1)S(1)}, bf16[160,896]{1,0:T(8,128)(2,1)S(1)}, u32[]{:S(2)}, u32[]{:S(2)}) collective-permute-start(bf16[160,896]{1,0:T(8,128)(2,1)S(1)} %slice.49), channel_id=1, source_target_pairs={{0,64},{32,96},{64,128},{96,160},{128,192},{160,224},{192,0},{224,... | collective-permute-start | bytes 860168 | tf_op jit(solution)/shard_map/ppermute | solution.py:15
  132.9 11.3 %collective-permute-start.15 = (bf16[160,896]{1,0:T(8,128)(2,1)S(1)}, bf16[160,896]{1,0:T(8,128)(2,1)S(1)}, u32[]{:S(2)}, u32[]{:S(2)}) collective-permute-start(bf16[160,896]{1,0:T(8,128)(2,1)S(1)} %slice.50), channel_id=1, source_target_pairs={{0,192},{32,224},{64,0},{96,32},{128,64},{160,96},{192,128},{224,1... | collective-permute-start | bytes 860168 | tf_op jit(solution)/shard_map/ppermute | solution.py:15
  138.3 18.2 %collective-permute-start.20 = (bf16[320,896]{1,0:T(8,128)(2,1)S(1)}, bf16[320,896]{1,0:T(8,128)(2,1)S(1)}, u32[]{:S(2)}, u32[]{:S(2)}) collective-permute-start(bf16[320,896]{1,0:T(8,128)(2,1)S(1)} %get-tuple-element.101), channel_id=1, source_target_pairs={{0,64},{32,96},{64,128},{96,160},{128,192},{160,224},{192,0},{224,... | collective-permute-start | bytes 1720328 | tf_op jit(solution)/shard_map/ppermute | solution.py:15
  139.2 17.3 %collective-permute-start.21 = (bf16[320,896]{1,0:T(8,128)(2,1)S(1)}, bf16[320,896]{1,0:T(8,128)(2,1)S(1)}, u32[]{:S(2)}, u32[]{:S(2)}) collective-permute-start(bf16[320,896]{1,0:T(8,128)(2,1)S(1)} %get-tuple-element.102), channel_id=1, source_target_pairs={{0,192},{32,224},{64,0},{96,32},{128,64},{160,96},{192,128},{224,1... | collective-permute-start | bytes 1720328 | tf_op jit(solution)/shard_map/ppermute | solution.py:15
  147.1 15.5 %collective-permute-start.18 = (bf16[160,896]{1,0:T(8,128)(2,1)S(1)}, bf16[160,896]{1,0:T(8,128)(2,1)S(1)}, u32[]{:S(2)}, u32[]{:S(2)}) collective-permute-start(bf16[160,896]{1,0:T(8,128)(2,1)S(1)} %get-tuple-element.97), channel_id=1, source_target_pairs={{0,64},{32,96},{64,128},{96,160},{128,192},{160,224},{192,0},{224,... | collective-permute-start | bytes 860168 | tf_op jit(solution)/shard_map/ppermute | solution.py:15
  148.0 14.7 %collective-permute-start.19 = (bf16[160,896]{1,0:T(8,128)(2,1)S(1)}, bf16[160,896]{1,0:T(8,128)(2,1)S(1)}, u32[]{:S(2)}, u32[]{:S(2)}) collective-permute-start(bf16[160,896]{1,0:T(8,128)(2,1)S(1)} %get-tuple-element.98), channel_id=1, source_target_pairs={{0,192},{32,224},{64,0},{96,32},{128,64},{160,96},{192,128},{224,1... | collective-permute-start | bytes 860168 | tf_op jit(solution)/shard_map/ppermute | solution.py:15
  152.0 42.9 %collective-permute-start.23 = (bf16[320,896]{1,0:T(8,128)(2,1)S(1)}, bf16[320,896]{1,0:T(8,128)(2,1)S(1)}, u32[]{:S(2)}, u32[]{:S(2)}) collective-permute-start(bf16[320,896]{1,0:T(8,128)(2,1)S(1)} %get-tuple-element.108), channel_id=1, source_target_pairs={{0,192},{32,224},{64,0},{96,32},{128,64},{160,96},{192,128},{224,1... | collective-permute-start | bytes 1720328 | tf_op jit(solution)/shard_map/ppermute | solution.py:15
  162.9 13.4 %collective-permute-start.25 = (bf16[320,896]{1,0:T(8,128)(2,1)S(1)}, bf16[320,896]{1,0:T(8,128)(2,1)S(1)}, u32[]{:S(2)}, u32[]{:S(2)}) collective-permute-start(bf16[320,896]{1,0:T(8,128)(2,1)S(1)} %get-tuple-element.113), channel_id=1, source_target_pairs={{0,64},{32,96},{64,128},{96,160},{128,192},{160,224},{192,0},{224,... | collective-permute-start | bytes 1720328 | tf_op jit(solution)/shard_map/ppermute | solution.py:15
  163.8 22.4 %collective-permute-start.26 = (bf16[320,896]{1,0:T(8,128)(2,1)S(1)}, bf16[320,896]{1,0:T(8,128)(2,1)S(1)}, u32[]{:S(2)}, u32[]{:S(2)}) collective-permute-start(bf16[320,896]{1,0:T(8,128)(2,1)S(1)} %get-tuple-element.114), channel_id=1, source_target_pairs={{0,192},{32,224},{64,0},{96,32},{128,64},{160,96},{192,128},{224,1... | collective-permute-start | bytes 1720328 | tf_op jit(solution)/shard_map/ppermute | solution.py:15
  165.8 29.1 %collective-permute-start.24 = (bf16[320,896]{1,0:T(8,128)(2,1)S(1)}, bf16[320,896]{1,0:T(8,128)(2,1)S(1)}, u32[]{:S(2)}, u32[]{:S(2)}) collective-permute-start(bf16[320,896]{1,0:T(8,128)(2,1)S(1)} %add_convert_fusion.5), channel_id=1, source_target_pairs={{0,32},{32,0},{64,96},{96,64},{128,160},{160,128},{192,224},{224,1... | collective-permute-start | bytes 1720328 | tf_op jit(solution)/shard_map/ppermute | solution.py:19
  168.1 26.8 %collective-permute-start.22 = (bf16[320,896]{1,0:T(8,128)(2,1)S(1)}, bf16[320,896]{1,0:T(8,128)(2,1)S(1)}, u32[]{:S(2)}, u32[]{:S(2)}) collective-permute-start(bf16[320,896]{1,0:T(8,128)(2,1)S(1)} %get-tuple-element.107), channel_id=1, source_target_pairs={{0,64},{32,96},{64,128},{96,160},{128,192},{160,224},{192,0},{224,... | collective-permute-start | bytes 1720328 | tf_op jit(solution)/shard_map/ppermute | solution.py:15
  186.2 14.0 %collective-permute-start.30 = (bf16[320,896]{1,0:T(8,128)(2,1)S(1)}, bf16[320,896]{1,0:T(8,128)(2,1)S(1)}, u32[]{:S(2)}, u32[]{:S(2)}) collective-permute-start(bf16[320,896]{1,0:T(8,128)(2,1)S(1)} %get-tuple-element.124), channel_id=1, source_target_pairs={{0,192},{32,224},{64,0},{96,32},{128,64},{160,96},{192,128},{224,1... | collective-permute-start | bytes 1720328 | tf_op jit(solution)/shard_map/ppermute | solution.py:15
  189.6 13.7 %collective-permute-start.29 = (bf16[320,896]{1,0:T(8,128)(2,1)S(1)}, bf16[320,896]{1,0:T(8,128)(2,1)S(1)}, u32[]{:S(2)}, u32[]{:S(2)}) collective-permute-start(bf16[320,896]{1,0:T(8,128)(2,1)S(1)} %get-tuple-element.122), channel_id=1, source_target_pairs={{0,64},{32,96},{64,128},{96,160},{128,192},{160,224},{192,0},{224,... | collective-permute-start | bytes 1720328 | tf_op jit(solution)/shard_map/ppermute | solution.py:15
  195.1 17.4 %collective-permute-start.28 = (bf16[320,896]{1,0:T(8,128)(2,1)S(1)}, bf16[320,896]{1,0:T(8,128)(2,1)S(1)}, u32[]{:S(2)}, u32[]{:S(2)}) collective-permute-start(bf16[320,896]{1,0:T(8,128)(2,1)S(1)} %add_convert_fusion.3), channel_id=1, source_target_pairs={{0,192},{32,224},{64,0},{96,32},{128,64},{160,96},{192,128},{224,1... | collective-permute-start | bytes 1720328 | tf_op jit(solution)/shard_map/ppermute | solution.py:15
  195.3 20.3 %collective-permute-start.27 = (bf16[320,896]{1,0:T(8,128)(2,1)S(1)}, bf16[320,896]{1,0:T(8,128)(2,1)S(1)}, u32[]{:S(2)}, u32[]{:S(2)}) collective-permute-start(bf16[320,896]{1,0:T(8,128)(2,1)S(1)} %add_convert_fusion.4), channel_id=1, source_target_pairs={{0,64},{32,96},{64,128},{96,160},{128,192},{160,224},{192,0},{224,... | collective-permute-start | bytes 1720328 | tf_op jit(solution)/shard_map/ppermute | solution.py:15
  197.1 23.3 %collective-permute-start.31 = (bf16[320,896]{1,0:T(8,128)(2,1)S(1)}, bf16[320,896]{1,0:T(8,128)(2,1)S(1)}, u32[]{:S(2)}, u32[]{:S(2)}) collective-permute-start(bf16[320,896]{1,0:T(8,128)(2,1)S(1)} %add_convert_fusion.1), channel_id=1, source_target_pairs={{0,32},{32,0},{64,96},{96,64},{128,160},{160,128},{192,224},{224,1... | collective-permute-start | bytes 1720328 | tf_op jit(solution)/shard_map/ppermute | solution.py:19
  222.6 4.2 %copy-start.12 = (f32[160,2]{0,1:T(2,128)S(1)}, f32[160,2]{0,1:T(2,128)}, u32[]{:S(2)}) copy-start(f32[160,2]{0,1:T(2,128)} %param.8) | copy-start | bytes 3844
  222.6 39.1 %all-to-all-start.1 = ((bf16[32,24,896]{2,1,0:T(8,128)(2,1)}), bf16[32,24,896]{2,1,0:T(8,128)(2,1)S(1)}, u32[]{:S(2)}, u32[]{:S(2)}) async-start(bf16[32,24,896]{2,1,0:T(8,128)(2,1)} %bitcast.16), calls=%async_computation.1 | async-start | bytes 2752512 | tf_op jit(solution)/shard_map/all_to_all | solution.py:37
where the time goes:
time: 264 us; the launch traced here: 263 us
  waiting for transfers between devices  171 us (65%)
  starting transfers between devices  56.9 us (22%)
  Pallas kernels  15.1 us (6%)
  local copies, waits for them, and re-layouts  10.9 us (4%)
  matrix products  6.97 us (3%)
    all_to_all x2, waiting for transfers between devices, exchange(): lax.all_to_all(rows.reshape(n_ep, PAD_PAIR, width), 'ep', 0, 0, tiled=True)  69.6 us
    ppermute x28, waiting for transfers between devices, move(): return lax.ppermute(x, 'rep', [(i, (i + 2 * by) % 8) for i in range(8)])  69 us
    ppermute x4, waiting for transfers between devices, swap(): return lax.ppermute(x, 'rep', [(i, i ^ 1) for i in range(8)])  32.6 us
    ppermute x28, starting transfers between devices, move(): return lax.ppermute(x, 'rep', [(i, (i + 2 * by) % 8) for i in range(8)])  32.5 us
    pallas_call x7, Pallas kernels, call(): pl.pallas_call(body, in_specs=[smem if a.ndim == 1 else vmem for a in arg...  15.1 us
    all_to_all x2, starting transfers between devices, exchange(): lax.all_to_all(rows.reshape(n_ep, PAD_PAIR, width), 'ep', 0, 0, tiled=True)  14.4 us
    ppermute x4, starting transfers between devices, swap(): return lax.ppermute(x, 'rep', [(i, i ^ 1) for i in range(8)])  10 us
    unnamed x26, local copies, waits for them, and re-layouts  9.72 us
  transfers between devices with their start and end apart: 34, of which 21 were waited for; matrix products, arithmetic and copies ran while one was open for 1% of the time, Pallas kernels for 6%

commit v1 on v0

--- a/solution.py
+++ b/solution.py
@@ -219,7 +219,7 @@
             w_down,
         )
 
-    lt, rb = move(top, 1), move(bottom, -1)
+    lt, rb = move(top, 1), move(after(bottom, top), -1)
     swap1 = swap(top)
     ft, fb = move(lt, 1), move(rb, -1)
     swap2 = swap(after(bottom, lt, rb))
@@ -273,11 +273,11 @@
     total = [pick(spread, add(t0, lt, rt, came1)), pick(spread, add(b0, lb, rb, came2))]
     back = exchange(jnp.concatenate(total, axis=0), n_ep)
 
-    columns = lax.broadcasted_iota(jnp.int32, (tokens.shape[0], n_ep * PAD_PAIR), 1)
-    out = sum(
-        weights[:, k : k + 1] * mm((columns == row[k][:, None]).astype(jnp.bfloat16), back)
-        for k in range(2)
-    )
+    count = tokens.shape[0]
+    columns = lax.broadcasted_iota(jnp.int32, (2 * count, n_ep * PAD_PAIR), 1)
+    choose = (columns == row.reshape(-1)[:, None]).astype(jnp.bfloat16)
+    chosen = mm(choose, back)
+    out = weights[:, :1] * chosen[:count] + weights[:, 1:] * chosen[count:]
     return out.astype(jnp.bfloat16)
 
 

time: 264 us -> 264 us (level)
  no operation moved by 1% of the time
where the time goes in v1:
time: 264 us; the launch traced here: 263 us
  waiting for transfers between devices  171 us (65%)
  starting transfers between devices  57.5 us (22%)
  Pallas kernels  15.1 us (6%)
  local copies, waits for them, and re-layouts  10.1 us (4%)
  matrix products  6.03 us (2%)
  other arithmetic  2.86 us (1%)
    all_to_all x2, waiting for transfers between devices, exchange(): lax.all_to_all(rows.reshape(n_ep, PAD_PAIR, width), 'ep', 0, 0, tiled=True)  69.6 us
    ppermute x28, waiting for transfers between devices, move(): return lax.ppermute(x, 'rep', [(i, (i + 2 * by) % 8) for i in range(8)])  69.3 us
    ppermute x28, starting transfers between devices, move(): return lax.ppermute(x, 'rep', [(i, (i + 2 * by) % 8) for i in range(8)])  33.2 us
    ppermute x4, waiting for transfers between devices, swap(): return lax.ppermute(x, 'rep', [(i, i ^ 1) for i in range(8)])  32.4 us
    pallas_call x7, Pallas kernels, call(): pl.pallas_call(body, in_specs=[smem if a.ndim == 1 else vmem for a in arg...  15.1 us
    all_to_all x2, starting transfers between devices, exchange(): lax.all_to_all(rows.reshape(n_ep, PAD_PAIR, width), 'ep', 0, 0, tiled=True)  14.4 us
    ppermute x4, starting transfers between devices, swap(): return lax.ppermute(x, 'rep', [(i, i ^ 1) for i in range(8)])  9.89 us
    unnamed x26, local copies, waits for them, and re-layouts  8.9 us
  transfers between devices with their start and end apart: 34, of which 21 were waited for; matrix products, arithmetic and copies ran while one was open for 1% of the time, Pallas kernels for 6%

profile of v1, /device:TPU:1, one launch (start us, length us, event | category | flops | bytes accessed | tf_op | source)
XLA Modules:
  0.0 263.3 jit_solution(28919132829951382)
XLA Ops:
  1.2 1.7 convolution_convert_fusion
  2.9 10.2 %all-to-all-start = ((bf16[32,24,896]{2,1,0:T(8,128)(2,1)}), bf16[32,24,896]{2,1,0:T(8,128)(2,1)S(1)}, u32[]{:S(2)}, u32[]{:S(2)}) async-start(bf16[32,24,896]{2,1,0:T(8,128)(2,1)} %bitcast.10), calls=%async_computation | async-start | bytes 2752512 | tf_op jit(solution)/shard_map/all_to_all | solution.py:37
  13.1 34.7 %all-to-all-done = bf16[32,24,896]{2,1,0:T(8,128)(2,1)S(1)} async-done(((bf16[32,24,896]{2,1,0:T(8,128)(2,1)}), bf16[32,24,896]{2,1,0:T(8,128)(2,1)S(1)}, u32[]{:S(2)}, u32[]{:S(2)}) %all-to-all-start) | async-done | bytes 1376288 | tf_op jit(solution)/shard_map/all_to_all | solution.py:37
  49.5 2.6 collective-permute-start.2
  52.0 4.2 %collective-permute-start.6 = (bf16[320,896]{1,0:T(8,128)(2,1)S(1)}, bf16[320,896]{1,0:T(8,128)(2,1)S(1)}, u32[]{:S(2)}, u32[]{:S(2)}) collective-permute-start(bf16[320,896]{1,0:T(8,128)(2,1)S(1)} %convolution_convert_fusion.4.refs_0_), channel_id=1, source_target_pairs={{0,32},{32,0},{64,96},{96,64},{128,160},{160,128},{192,224},{224,1... | collective-permute-start | bytes 1720328 | tf_op jit(solution)/shard_map/ppermute | solution.py:19
  56.3 7.7 %collective-permute-done.2.refs_3_ = bf16[320,896]{1,0:T(8,128)(2,1)} collective-permute-done((bf16[320,896]{1,0:T(8,128)(2,1)S(1)}, bf16[320,896]{1,0:T(8,128)(2,1)}, u32[]{:S(2)}, u32[]{:S(2)}) %collective-permute-start.2) | collective-permute-done | bytes 573472 | tf_op jit(solution)/shard_map/ppermute | solution.py:15
  65.0 2.2 collective-permute-done.refs_4_
  67.5 1.5 collective-permute-start.5
  69.0 13.5 %collective-permute-done.6.refs_0_ = bf16[320,896]{1,0:T(8,128)(2,1)S(1)} collective-permute-done((bf16[320,896]{1,0:T(8,128)(2,1)S(1)}, bf16[320,896]{1,0:T(8,128)(2,1)S(1)}, u32[]{:S(2)}, u32[]{:S(2)}) %collective-permute-start.6) | collective-permute-done | bytes 573472 | tf_op jit(solution)/shard_map/ppermute | solution.py:19
  84.1 2.6 %collective-permute-start.7 = (bf16[320,896]{1,0:T(8,128)(2,1)S(1)}, bf16[320,896]{1,0:T(8,128)(2,1)S(1)}, u32[]{:S(2)}, u32[]{:S(2)}) collective-permute-start(bf16[320,896]{1,0:T(8,128)(2,1)S(1)} %collective-permute-done.6.refs_0_), channel_id=1, source_target_pairs={{0,192},{32,224},{64,0},{96,32},{128,64},{160,96},{192,128},{224,1... | collective-permute-start | bytes 1720328 | tf_op jit(solution)/shard_map/ppermute | solution.py:15
  86.7 2.2 collective-permute-start.11
  89.0 3.5 %collective-permute-done.5.refs_7_ = bf16[320,896]{1,0:T(8,128)(2,1)} collective-permute-done((bf16[320,896]{1,0:T(8,128)(2,1)}, bf16[320,896]{1,0:T(8,128)(2,1)}, u32[]{:S(2)}, u32[]{:S(2)}) %collective-permute-start.5) | collective-permute-done | bytes 573472 | tf_op jit(solution)/shard_map/ppermute | solution.py:15
  92.4 2.0 copy-done.2
  94.5 2.0 copy-done.4
  99.7 4.8 %shard_map.64 = (f32[320,256]{1,0:T(8,128)S(1)}, f32[320,256]{1,0:T(8,128)S(1)}, f32[320,256]{1,0:T(8,128)S(1)}, f32[320,256]{1,0:T(8,128)S(1)}) custom-call(s32[8]{0:T(128)S(1)} %stack.35.idx, bf16[320,896]{1,0:T(8,128)(2,1)S(1)} %copy-done.7, bf16[320,896]{1,0:T(8,128)(2,1)S(1)} %convolution_convert_fusion.3.refs_1_, bf16[320,896]{1,0:T(8,128)(2,1)S(1)} %copy-done.11, ...), custom_call_target="tpu_custom_call" | custom-call | flops 2348810240 | bytes 13238304 | tf_op jit(solution)/shard_map/pallas_call | solution.py:151
  104.6 2.1 collective-permute-start.10
  106.9 9.8 %collective-permute-done.11.refs_0_ = bf16[320,896]{1,0:T(8,128)(2,1)S(1)} collective-permute-done((bf16[320,896]{1,0:T(8,128)(2,1)S(1)}, bf16[320,896]{1,0:T(8,128)(2,1)S(1)}, u32[]{:S(2)}, u32[]{:S(2)}) %collective-permute-start.11) | collective-permute-done | bytes 573472 | tf_op jit(solution)/shard_map/ppermute | solution.py:19
  116.6 2.7 %collective-permute-start.13 = (bf16[320,896]{1,0:T(8,128)(2,1)S(1)}, bf16[320,896]{1,0:T(8,128)(2,1)S(1)}, u32[]{:S(2)}, u32[]{:S(2)}) collective-permute-start(bf16[320,896]{1,0:T(8,128)(2,1)S(1)} %collective-permute-done.11.refs_0_), channel_id=1, source_target_pairs={{0,192},{32,224},{64,0},{96,32},{128,64},{160,96},{192,128},{224,1... | collective-permute-start | bytes 1720328 | tf_op jit(solution)/shard_map/ppermute | solution.py:15
  119.3 2.9 %shard_map.65 = (bf16[320,256]{1,0:T(8,128)(2,1)S(1)}, bf16[160,896]{1,0:T(8,128)(2,1)S(1)}, bf16[160,896]{1,0:T(8,128)(2,1)S(1)}) custom-call(s32[8]{0:T(128)S(1)} %stack.35.idx, f32[320,256]{1,0:T(8,128)S(1)} %get-tuple-element.72.g_in, f32[320,256]{1,0:T(8,128)S(1)} %get-tuple-element.73.u_in, bf16[320,896]{1,0:T(8,128)(2,1)S(1)} %collective-permute-done.6.refs_0_, ...), custom_call_target="tpu_custom_call" | custom-call | flops 1321205760 | bytes 14696480 | tf_op jit(solution)/shard_map/pallas_call | solution.py:151
  122.3 2.7 %collective-permute-start.17 = (bf16[160,896]{1,0:T(8,128)(2,1)S(1)}, bf16[160,896]{1,0:T(8,128)(2,1)S(1)}, u32[]{:S(2)}, u32[]{:S(2)}) collective-permute-start(bf16[160,896]{1,0:T(8,128)(2,1)S(1)} %get-tuple-element.89), channel_id=1, source_target_pairs={{0,192},{32,224},{64,0},{96,32},{128,64},{160,96},{192,128},{224,1... | collective-permute-start | bytes 860168 | tf_op jit(solution)/shard_map/ppermute | solution.py:15
  125.0 6.9 %collective-permute-done.12.refs_2_ = bf16[320,896]{1,0:T(8,128)(2,1)S(1)} collective-permute-done((bf16[320,896]{1,0:T(8,128)(2,1)S(1)}, bf16[320,896]{1,0:T(8,128)(2,1)S(1)}, u32[]{:S(2)}, u32[]{:S(2)}) %collective-permute-start.12) | collective-permute-done | bytes 573472 | tf_op jit(solution)/shard_map/ppermute | solution.py:15
  132.9 1.9 collective-permute-start.15
  134.8 2.1 shard_map.66
  136.9 1.1 collective-permute-done.16.top
  139.1 1.9 collective-permute-start.21
  141.0 3.2 %collective-permute-done.14.refs_3_ = bf16[160,896]{1,0:T(8,128)(2,1)S(1)} collective-permute-done((bf16[160,896]{1,0:T(8,128)(2,1)S(1)}, bf16[160,896]{1,0:T(8,128)(2,1)S(1)}, u32[]{:S(2)}, u32[]{:S(2)}) %collective-permute-start.14) | collective-permute-done | bytes 286752 | tf_op jit(solution)/shard_map/ppermute | solution.py:15
  144.2 2.9 %shard_map.67 = (bf16[320,256]{1,0:T(8,128)(2,1)S(1)}, bf16[160,896]{1,0:T(8,128)(2,1)S(1)}, bf16[160,896]{1,0:T(8,128)(2,1)S(1)}) custom-call(s32[8]{0:T(128)S(1)} %stack.35.idx, f32[320,256]{1,0:T(8,128)S(1)} %get-tuple-element.84.g_in, f32[320,256]{1,0:T(8,128)S(1)} %get-tuple-element.85.u_in, bf16[320,896]{1,0:T(8,128)(2,1)S(1)} %collective-permute-done.11.refs_0_, ...), custom_call_target="tpu_custom_call" | custom-call | flops 1321205760 | bytes 14696480 | tf_op jit(solution)/shard_map/pallas_call | solution.py:151
  148.0 1.9 collective-permute-start.19
  149.8 2.1 shard_map.69
  151.9 1.4 collective-permute-start.23
  153.4 3.1 %collective-permute-done.20 = bf16[320,896]{1,0:T(8,128)(2,1)S(1)} collective-permute-done((bf16[320,896]{1,0:T(8,128)(2,1)S(1)}, bf16[320,896]{1,0:T(8,128)(2,1)S(1)}, u32[]{:S(2)}, u32[]{:S(2)}) %collective-permute-start.20) | collective-permute-done | bytes 573472 | tf_op jit(solution)/shard_map/ppermute | solution.py:15
  156.5 6.1 %collective-permute-done.18.top = bf16[160,896]{1,0:T(8,128)(2,1)S(1)} collective-permute-done((bf16[160,896]{1,0:T(8,128)(2,1)S(1)}, bf16[160,896]{1,0:T(8,128)(2,1)S(1)}, u32[]{:S(2)}, u32[]{:S(2)}) %collective-permute-start.18) | collective-permute-done | bytes 286752 | tf_op jit(solution)/shard_map/ppermute | solution.py:15
  163.7 1.9 collective-permute-start.26
  165.8 2.3 collective-permute-start.24
  168.1 8.2 %collective-permute-done.25 = bf16[320,896]{1,0:T(8,128)(2,1)S(1)} collective-permute-done((bf16[320,896]{1,0:T(8,128)(2,1)S(1)}, bf16[320,896]{1,0:T(8,128)(2,1)S(1)}, u32[]{:S(2)}, u32[]{:S(2)}) %collective-permute-start.25) | collective-permute-done | bytes 573472 | tf_op jit(solution)/shard_map/ppermute | solution.py:15
  176.3 9.9 %collective-permute-done.26 = bf16[320,896]{1,0:T(8,128)(2,1)S(1)} collective-permute-done((bf16[320,896]{1,0:T(8,128)(2,1)S(1)}, bf16[320,896]{1,0:T(8,128)(2,1)S(1)}, u32[]{:S(2)}, u32[]{:S(2)}) %collective-permute-start.26) | collective-permute-done | bytes 573472 | tf_op jit(solution)/shard_map/ppermute | solution.py:15
  186.1 3.4 %collective-permute-start.30 = (bf16[320,896]{1,0:T(8,128)(2,1)S(1)}, bf16[320,896]{1,0:T(8,128)(2,1)S(1)}, u32[]{:S(2)}, u32[]{:S(2)}) collective-permute-start(bf16[320,896]{1,0:T(8,128)(2,1)S(1)} %get-tuple-element.126), channel_id=1, source_target_pairs={{0,192},{32,224},{64,0},{96,32},{128,64},{160,96},{192,128},{224,1... | collective-permute-start | bytes 1720328 | tf_op jit(solution)/shard_map/ppermute | solution.py:15
  189.6 5.3 %collective-permute-done.24 = bf16[320,896]{1,0:T(8,128)(2,1)S(1)} collective-permute-done((bf16[320,896]{1,0:T(8,128)(2,1)S(1)}, bf16[320,896]{1,0:T(8,128)(2,1)S(1)}, u32[]{:S(2)}, u32[]{:S(2)}) %collective-permute-start.24) | collective-permute-done | bytes 573472 | tf_op jit(solution)/shard_map/ppermute | solution.py:19
  195.3 1.5 collective-permute-start.27
  197.1 1.3 collective-permute-start.31
  198.3 1.9 collective-permute-done.30
  200.2 3.1 %collective-permute-done.29 = bf16[320,896]{1,0:T(8,128)(2,1)S(1)} collective-permute-done((bf16[320,896]{1,0:T(8,128)(2,1)S(1)}, bf16[320,896]{1,0:T(8,128)(2,1)S(1)}, u32[]{:S(2)}, u32[]{:S(2)}) %collective-permute-start.29) | collective-permute-done | bytes 573472 | tf_op jit(solution)/shard_map/ppermute | solution.py:15
  203.3 9.2 %collective-permute-done.28 = bf16[320,896]{1,0:T(8,128)(2,1)S(1)} collective-permute-done((bf16[320,896]{1,0:T(8,128)(2,1)S(1)}, bf16[320,896]{1,0:T(8,128)(2,1)S(1)}, u32[]{:S(2)}, u32[]{:S(2)}) %collective-permute-start.28) | collective-permute-done | bytes 573472 | tf_op jit(solution)/shard_map/ppermute | solution.py:15
  212.5 3.1 %collective-permute-done.27 = bf16[320,896]{1,0:T(8,128)(2,1)S(1)} collective-permute-done((bf16[320,896]{1,0:T(8,128)(2,1)S(1)}, bf16[320,896]{1,0:T(8,128)(2,1)S(1)}, u32[]{:S(2)}, u32[]{:S(2)}) %collective-permute-start.27) | collective-permute-done | bytes 573472 | tf_op jit(solution)/shard_map/ppermute | solution.py:15
  216.5 3.8 %collective-permute-done.31 = bf16[320,896]{1,0:T(8,128)(2,1)S(1)} collective-permute-done((bf16[320,896]{1,0:T(8,128)(2,1)S(1)}, bf16[320,896]{1,0:T(8,128)(2,1)S(1)}, u32[]{:S(2)}, u32[]{:S(2)}) %collective-permute-start.31) | collective-permute-done | bytes 573472 | tf_op jit(solution)/shard_map/ppermute | solution.py:19
  221.3 1.2 pad_maximum_fusion
  222.6 4.2 %all-to-all-start.1 = ((bf16[32,24,896]{2,1,0:T(8,128)(2,1)}), bf16[32,24,896]{2,1,0:T(8,128)(2,1)S(1)}, u32[]{:S(2)}, u32[]{:S(2)}) async-start(bf16[32,24,896]{2,1,0:T(8,128)(2,1)} %bitcast.16), calls=%async_computation.1 | async-start | bytes 2752512 | tf_op jit(solution)/shard_map/all_to_all | solution.py:37
  226.8 34.9 %all-to-all-done.1 = bf16[32,24,896]{2,1,0:T(8,128)(2,1)S(1)} async-done(((bf16[32,24,896]{2,1,0:T(8,128)(2,1)}), bf16[32,24,896]{2,1,0:T(8,128)(2,1)S(1)}, u32[]{:S(2)}, u32[]{:S(2)}) %all-to-all-start.1) | async-done | bytes 1376288 | tf_op jit(solution)/shard_map/all_to_all | solution.py:37
  (80 shorter events, 17.7 us)
Async XLA Ops:
  0.0 1.2 copy-start
  2.9 45.0 %all-to-all-start = ((bf16[32,24,896]{2,1,0:T(8,128)(2,1)}), bf16[32,24,896]{2,1,0:T(8,128)(2,1)S(1)}, u32[]{:S(2)}, u32[]{:S(2)}) async-start(bf16[32,24,896]{2,1,0:T(8,128)(2,1)} %bitcast.10), calls=%async_computation | async-start | bytes 2752512 | tf_op jit(solution)/shard_map/all_to_all | solution.py:37
  48.7 33.7 %copy-start.6 = (bf16[320,896]{1,0:T(8,128)(2,1)}, bf16[320,896]{1,0:T(8,128)(2,1)S(1)}, u32[]{:S(2)}) copy-start(bf16[320,896]{1,0:T(8,128)(2,1)S(1)} %convolution_convert_fusion.4.refs_0_) | copy-start | bytes 1720324
  49.5 14.5 %collective-permute-start.2 = (bf16[320,896]{1,0:T(8,128)(2,1)S(1)}, bf16[320,896]{1,0:T(8,128)(2,1)}, u32[]{:S(2)}, u32[]{:S(2)}) collective-permute-start(bf16[320,896]{1,0:T(8,128)(2,1)S(1)} %convolution_convert_fusion.3.refs_1_), channel_id=1, source_target_pairs={{0,192},{32,224},{64,0},{96,32},{128,64},{160,96},{192,128},{224,1... | collective-permute-start | bytes 1720328 | tf_op jit(solution)/shard_map/ppermute | solution.py:15
  52.0 15.1 %collective-permute-start = (bf16[320,896]{1,0:T(8,128)(2,1)S(1)}, bf16[320,896]{1,0:T(8,128)(2,1)}, u32[]{:S(2)}, u32[]{:S(2)}) collective-permute-start(bf16[320,896]{1,0:T(8,128)(2,1)S(1)} %convolution_convert_fusion.4.refs_0_), channel_id=1, source_target_pairs={{0,64},{32,96},{64,128},{96,160},{128,192},{160,224},{192,0},{224,... | collective-permute-start | bytes 1720328 | tf_op jit(solution)/shard_map/ppermute | solution.py:15
  52.0 30.4 %collective-permute-start.6 = (bf16[320,896]{1,0:T(8,128)(2,1)S(1)}, bf16[320,896]{1,0:T(8,128)(2,1)S(1)}, u32[]{:S(2)}, u32[]{:S(2)}) collective-permute-start(bf16[320,896]{1,0:T(8,128)(2,1)S(1)} %convolution_convert_fusion.4.refs_0_), channel_id=1, source_target_pairs={{0,32},{32,0},{64,96},{96,64},{128,160},{160,128},{192,224},{224,1... | collective-permute-start | bytes 1720328 | tf_op jit(solution)/shard_map/ppermute | solution.py:19
  64.0 18.5 %collective-permute-start.3 = (bf16[320,896]{1,0:T(8,128)(2,1)S(1)}, bf16[320,896]{1,0:T(8,128)(2,1)S(1)}, u32[]{:S(2)}, u32[]{:S(2)}) collective-permute-start(bf16[320,896]{1,0:T(8,128)(2,1)S(1)} %convolution_convert_fusion.3.refs_1_), channel_id=1, source_target_pairs={{0,64},{32,96},{64,128},{96,160},{128,192},{160,224},{192,0},{224,... | collective-permute-start | bytes 1720328 | tf_op jit(solution)/shard_map/ppermute | solution.py:15
  67.2 16.1 %collective-permute-start.1 = (bf16[320,896]{1,0:T(8,128)(2,1)S(1)}, bf16[320,896]{1,0:T(8,128)(2,1)S(1)}, u32[]{:S(2)}, u32[]{:S(2)}) collective-permute-start(bf16[320,896]{1,0:T(8,128)(2,1)S(1)} %convolution_convert_fusion.4.refs_0_), channel_id=1, source_target_pairs={{0,192},{32,224},{64,0},{96,32},{128,64},{160,96},{192,128},{224,1... | collective-permute-start | bytes 1720328 | tf_op jit(solution)/shard_map/ppermute | solution.py:15
  67.5 24.9 %collective-permute-start.5 = (bf16[320,896]{1,0:T(8,128)(2,1)}, bf16[320,896]{1,0:T(8,128)(2,1)}, u32[]{:S(2)}, u32[]{:S(2)}) collective-permute-start(bf16[320,896]{1,0:T(8,128)(2,1)} %collective-permute-done.2.refs_3_), channel_id=1, source_target_pairs={{0,192},{32,224},{64,0},{96,32},{128,64},{160,96},{192,128},{224,1... | collective-permute-start | bytes 1720328 | tf_op jit(solution)/shard_map/ppermute | solution.py:15
  69.0 23.5 %collective-permute-start.4 = (bf16[320,896]{1,0:T(8,128)(2,1)}, bf16[320,896]{1,0:T(8,128)(2,1)}, u32[]{:S(2)}, u32[]{:S(2)}) collective-permute-start(bf16[320,896]{1,0:T(8,128)(2,1)} %collective-permute-done.refs_4_), channel_id=1, source_target_pairs={{0,64},{32,96},{64,128},{96,160},{128,192},{160,224},{192,0},{224,... | collective-permute-start | bytes 1720328 | tf_op jit(solution)/shard_map/ppermute | solution.py:15
  82.4 0.8 copy-start.8
  83.3 0.8 copy-start.10
  84.1 20.5 %collective-permute-start.7 = (bf16[320,896]{1,0:T(8,128)(2,1)S(1)}, bf16[320,896]{1,0:T(8,128)(2,1)S(1)}, u32[]{:S(2)}, u32[]{:S(2)}) collective-permute-start(bf16[320,896]{1,0:T(8,128)(2,1)S(1)} %collective-permute-done.6.refs_0_), channel_id=1, source_target_pairs={{0,192},{32,224},{64,0},{96,32},{128,64},{160,96},{192,128},{224,1... | collective-permute-start | bytes 1720328 | tf_op jit(solution)/shard_map/ppermute | solution.py:15
  86.7 20.0 %collective-permute-start.8 = (bf16[320,896]{1,0:T(8,128)(2,1)S(1)}, bf16[320,896]{1,0:T(8,128)(2,1)S(1)}, u32[]{:S(2)}, u32[]{:S(2)}) collective-permute-start(bf16[320,896]{1,0:T(8,128)(2,1)S(1)} %collective-permute-done.6.refs_0_), channel_id=1, source_target_pairs={{0,64},{32,96},{64,128},{96,160},{128,192},{160,224},{192,0},{224,... | collective-permute-start | bytes 1720328 | tf_op jit(solution)/shard_map/ppermute | solution.py:15
  86.7 29.9 %collective-permute-start.11 = (bf16[320,896]{1,0:T(8,128)(2,1)S(1)}, bf16[320,896]{1,0:T(8,128)(2,1)S(1)}, u32[]{:S(2)}, u32[]{:S(2)}) collective-permute-start(bf16[320,896]{1,0:T(8,128)(2,1)S(1)} %convolution_convert_fusion.3.refs_1_), channel_id=1, source_target_pairs={{0,32},{32,0},{64,96},{96,64},{128,160},{160,128},{192,224},{224,1... | collective-permute-start | bytes 1720328 | tf_op jit(solution)/shard_map/ppermute | solution.py:19
  92.4 2.0 copy-start.2
  94.5 2.0 copy-start.4
  96.5 1.1 copy-start.7
  97.6 1.1 copy-start.9
  98.6 1.1 copy-start.11
  99.7 19.6 %copy-start.1 = (bf16[1,256,7168]{2,1,0:T(8,128)(2,1)S(1)}, bf16[1,256,7168]{2,1,0:T(8,128)(2,1)}, u32[]{:S(2)}) copy-start(bf16[1,256,7168]{2,1,0:T(8,128)(2,1)} %param.11) | copy-start | bytes 11010052
  99.7 19.6 %copy-start.3 = (bf16[1,7168,256]{2,1,0:T(8,128)(2,1)S(1)}, bf16[1,7168,256]{2,1,0:T(8,128)(2,1)}, u32[]{:S(2)}) copy-start(bf16[1,7168,256]{2,1,0:T(8,128)(2,1)} %param.9) | copy-start | bytes 11010052
  99.7 19.7 %copy-start.5 = (bf16[1,7168,256]{2,1,0:T(8,128)(2,1)S(1)}, bf16[1,7168,256]{2,1,0:T(8,128)(2,1)}, u32[]{:S(2)}) copy-start(bf16[1,7168,256]{2,1,0:T(8,128)(2,1)} %param.10) | copy-start | bytes 11010052
  104.6 14.7 %collective-permute-start.10 = (bf16[160,896]{1,0:T(8,128)(2,1)S(1)}, bf16[160,896]{1,0:T(8,128)(2,1)S(1)}, u32[]{:S(2)}, u32[]{:S(2)}) collective-permute-start(bf16[160,896]{1,0:T(8,128)(2,1)S(1)} %slice.61), channel_id=1, source_target_pairs={{0,192},{32,224},{64,0},{96,32},{128,64},{160,96},{192,128},{224,1... | collective-permute-start | bytes 860168 | tf_op jit(solution)/shard_map/ppermute | solution.py:15
  106.8 12.5 %collective-permute-start.9 = (bf16[160,896]{1,0:T(8,128)(2,1)S(1)}, bf16[160,896]{1,0:T(8,128)(2,1)S(1)}, u32[]{:S(2)}, u32[]{:S(2)}) collective-permute-start(bf16[160,896]{1,0:T(8,128)(2,1)S(1)} %slice.60), channel_id=1, source_target_pairs={{0,64},{32,96},{64,128},{96,160},{128,192},{160,224},{192,0},{224,... | collective-permute-start | bytes 860168 | tf_op jit(solution)/shard_map/ppermute | solution.py:15
  116.6 15.3 %collective-permute-start.12 = (bf16[320,896]{1,0:T(8,128)(2,1)S(1)}, bf16[320,896]{1,0:T(8,128)(2,1)S(1)}, u32[]{:S(2)}, u32[]{:S(2)}) collective-permute-start(bf16[320,896]{1,0:T(8,128)(2,1)S(1)} %collective-permute-done.11.refs_0_), channel_id=1, source_target_pairs={{0,64},{32,96},{64,128},{96,160},{128,192},{160,224},{192,0},{224,... | collective-permute-start | bytes 1720328 | tf_op jit(solution)/shard_map/ppermute | solution.py:15
  116.6 15.3 %collective-permute-start.13 = (bf16[320,896]{1,0:T(8,128)(2,1)S(1)}, bf16[320,896]{1,0:T(8,128)(2,1)S(1)}, u32[]{:S(2)}, u32[]{:S(2)}) collective-permute-start(bf16[320,896]{1,0:T(8,128)(2,1)S(1)} %collective-permute-done.11.refs_0_), channel_id=1, source_target_pairs={{0,192},{32,224},{64,0},{96,32},{128,64},{160,96},{192,128},{224,1... | collective-permute-start | bytes 1720328 | tf_op jit(solution)/shard_map/ppermute | solution.py:15
  122.2 15.8 %collective-permute-start.16 = (bf16[160,896]{1,0:T(8,128)(2,1)S(1)}, bf16[160,896]{1,0:T(8,128)(2,1)S(1)}, u32[]{:S(2)}, u32[]{:S(2)}) collective-permute-start(bf16[160,896]{1,0:T(8,128)(2,1)S(1)} %get-tuple-element.88), channel_id=1, source_target_pairs={{0,64},{32,96},{64,128},{96,160},{128,192},{160,224},{192,0},{224,... | collective-permute-start | bytes 860168 | tf_op jit(solution)/shard_map/ppermute | solution.py:15
  122.3 15.7 %collective-permute-start.17 = (bf16[160,896]{1,0:T(8,128)(2,1)S(1)}, bf16[160,896]{1,0:T(8,128)(2,1)S(1)}, u32[]{:S(2)}, u32[]{:S(2)}) collective-permute-start(bf16[160,896]{1,0:T(8,128)(2,1)S(1)} %get-tuple-element.89), channel_id=1, source_target_pairs={{0,192},{32,224},{64,0},{96,32},{128,64},{160,96},{192,128},{224,1... | collective-permute-start | bytes 860168 | tf_op jit(solution)/shard_map/ppermute | solution.py:15
  131.9 12.3 %collective-permute-start.14 = (bf16[160,896]{1,0:T(8,128)(2,1)S(1)}, bf16[160,896]{1,0:T(8,128)(2,1)S(1)}, u32[]{:S(2)}, u32[]{:S(2)}) collective-permute-start(bf16[160,896]{1,0:T(8,128)(2,1)S(1)} %slice.53), channel_id=1, source_target_pairs={{0,64},{32,96},{64,128},{96,160},{128,192},{160,224},{192,0},{224,... | collective-permute-start | bytes 860168 | tf_op jit(solution)/shard_map/ppermute | solution.py:15
  132.9 11.3 %collective-permute-start.15 = (bf16[160,896]{1,0:T(8,128)(2,1)S(1)}, bf16[160,896]{1,0:T(8,128)(2,1)S(1)}, u32[]{:S(2)}, u32[]{:S(2)}) collective-permute-start(bf16[160,896]{1,0:T(8,128)(2,1)S(1)} %slice.54), channel_id=1, source_target_pairs={{0,192},{32,224},{64,0},{96,32},{128,64},{160,96},{192,128},{224,1... | collective-permute-start | bytes 860168 | tf_op jit(solution)/shard_map/ppermute | solution.py:15
  138.2 18.2 %collective-permute-start.20 = (bf16[320,896]{1,0:T(8,128)(2,1)S(1)}, bf16[320,896]{1,0:T(8,128)(2,1)S(1)}, u32[]{:S(2)}, u32[]{:S(2)}) collective-permute-start(bf16[320,896]{1,0:T(8,128)(2,1)S(1)} %get-tuple-element.103), channel_id=1, source_target_pairs={{0,64},{32,96},{64,128},{96,160},{128,192},{160,224},{192,0},{224,... | collective-permute-start | bytes 1720328 | tf_op jit(solution)/shard_map/ppermute | solution.py:15
  139.1 17.3 %collective-permute-start.21 = (bf16[320,896]{1,0:T(8,128)(2,1)S(1)}, bf16[320,896]{1,0:T(8,128)(2,1)S(1)}, u32[]{:S(2)}, u32[]{:S(2)}) collective-permute-start(bf16[320,896]{1,0:T(8,128)(2,1)S(1)} %get-tuple-element.104), channel_id=1, source_target_pairs={{0,192},{32,224},{64,0},{96,32},{128,64},{160,96},{192,128},{224,1... | collective-permute-start | bytes 1720328 | tf_op jit(solution)/shard_map/ppermute | solution.py:15
  147.1 15.6 %collective-permute-start.18 = (bf16[160,896]{1,0:T(8,128)(2,1)S(1)}, bf16[160,896]{1,0:T(8,128)(2,1)S(1)}, u32[]{:S(2)}, u32[]{:S(2)}) collective-permute-start(bf16[160,896]{1,0:T(8,128)(2,1)S(1)} %get-tuple-element.99), channel_id=1, source_target_pairs={{0,64},{32,96},{64,128},{96,160},{128,192},{160,224},{192,0},{224,... | collective-permute-start | bytes 860168 | tf_op jit(solution)/shard_map/ppermute | solution.py:15
  148.0 14.7 %collective-permute-start.19 = (bf16[160,896]{1,0:T(8,128)(2,1)S(1)}, bf16[160,896]{1,0:T(8,128)(2,1)S(1)}, u32[]{:S(2)}, u32[]{:S(2)}) collective-permute-start(bf16[160,896]{1,0:T(8,128)(2,1)S(1)} %get-tuple-element.100), channel_id=1, source_target_pairs={{0,192},{32,224},{64,0},{96,32},{128,64},{160,96},{192,128},{224,1... | collective-permute-start | bytes 860168 | tf_op jit(solution)/shard_map/ppermute | solution.py:15
  151.9 43.0 %collective-permute-start.23 = (bf16[320,896]{1,0:T(8,128)(2,1)S(1)}, bf16[320,896]{1,0:T(8,128)(2,1)S(1)}, u32[]{:S(2)}, u32[]{:S(2)}) collective-permute-start(bf16[320,896]{1,0:T(8,128)(2,1)S(1)} %get-tuple-element.110), channel_id=1, source_target_pairs={{0,192},{32,224},{64,0},{96,32},{128,64},{160,96},{192,128},{224,1... | collective-permute-start | bytes 1720328 | tf_op jit(solution)/shard_map/ppermute | solution.py:15
  162.8 13.4 %collective-permute-start.25 = (bf16[320,896]{1,0:T(8,128)(2,1)S(1)}, bf16[320,896]{1,0:T(8,128)(2,1)S(1)}, u32[]{:S(2)}, u32[]{:S(2)}) collective-permute-start(bf16[320,896]{1,0:T(8,128)(2,1)S(1)} %get-tuple-element.115), channel_id=1, source_target_pairs={{0,64},{32,96},{64,128},{96,160},{128,192},{160,224},{192,0},{224,... | collective-permute-start | bytes 1720328 | tf_op jit(solution)/shard_map/ppermute | solution.py:15
  163.7 22.4 %collective-permute-start.26 = (bf16[320,896]{1,0:T(8,128)(2,1)S(1)}, bf16[320,896]{1,0:T(8,128)(2,1)S(1)}, u32[]{:S(2)}, u32[]{:S(2)}) collective-permute-start(bf16[320,896]{1,0:T(8,128)(2,1)S(1)} %get-tuple-element.116), channel_id=1, source_target_pairs={{0,192},{32,224},{64,0},{96,32},{128,64},{160,96},{192,128},{224,1... | collective-permute-start | bytes 1720328 | tf_op jit(solution)/shard_map/ppermute | solution.py:15
  165.8 29.1 %collective-permute-start.24 = (bf16[320,896]{1,0:T(8,128)(2,1)S(1)}, bf16[320,896]{1,0:T(8,128)(2,1)S(1)}, u32[]{:S(2)}, u32[]{:S(2)}) collective-permute-start(bf16[320,896]{1,0:T(8,128)(2,1)S(1)} %add_convert_fusion.5), channel_id=1, source_target_pairs={{0,32},{32,0},{64,96},{96,64},{128,160},{160,128},{192,224},{224,1... | collective-permute-start | bytes 1720328 | tf_op jit(solution)/shard_map/ppermute | solution.py:19
  168.1 26.8 %collective-permute-start.22 = (bf16[320,896]{1,0:T(8,128)(2,1)S(1)}, bf16[320,896]{1,0:T(8,128)(2,1)S(1)}, u32[]{:S(2)}, u32[]{:S(2)}) collective-permute-start(bf16[320,896]{1,0:T(8,128)(2,1)S(1)} %get-tuple-element.109), channel_id=1, source_target_pairs={{0,64},{32,96},{64,128},{96,160},{128,192},{160,224},{192,0},{224,... | collective-permute-start | bytes 1720328 | tf_op jit(solution)/shard_map/ppermute | solution.py:15
  186.1 14.0 %collective-permute-start.30 = (bf16[320,896]{1,0:T(8,128)(2,1)S(1)}, bf16[320,896]{1,0:T(8,128)(2,1)S(1)}, u32[]{:S(2)}, u32[]{:S(2)}) collective-permute-start(bf16[320,896]{1,0:T(8,128)(2,1)S(1)} %get-tuple-element.126), channel_id=1, source_target_pairs={{0,192},{32,224},{64,0},{96,32},{128,64},{160,96},{192,128},{224,1... | collective-permute-start | bytes 1720328 | tf_op jit(solution)/shard_map/ppermute | solution.py:15
  189.6 13.7 %collective-permute-start.29 = (bf16[320,896]{1,0:T(8,128)(2,1)S(1)}, bf16[320,896]{1,0:T(8,128)(2,1)S(1)}, u32[]{:S(2)}, u32[]{:S(2)}) collective-permute-start(bf16[320,896]{1,0:T(8,128)(2,1)S(1)} %get-tuple-element.124), channel_id=1, source_target_pairs={{0,64},{32,96},{64,128},{96,160},{128,192},{160,224},{192,0},{224,... | collective-permute-start | bytes 1720328 | tf_op jit(solution)/shard_map/ppermute | solution.py:15
  195.1 17.4 %collective-permute-start.28 = (bf16[320,896]{1,0:T(8,128)(2,1)S(1)}, bf16[320,896]{1,0:T(8,128)(2,1)S(1)}, u32[]{:S(2)}, u32[]{:S(2)}) collective-permute-start(bf16[320,896]{1,0:T(8,128)(2,1)S(1)} %add_convert_fusion.3), channel_id=1, source_target_pairs={{0,192},{32,224},{64,0},{96,32},{128,64},{160,96},{192,128},{224,1... | collective-permute-start | bytes 1720328 | tf_op jit(solution)/shard_map/ppermute | solution.py:15
  195.3 20.3 %collective-permute-start.27 = (bf16[320,896]{1,0:T(8,128)(2,1)S(1)}, bf16[320,896]{1,0:T(8,128)(2,1)S(1)}, u32[]{:S(2)}, u32[]{:S(2)}) collective-permute-start(bf16[320,896]{1,0:T(8,128)(2,1)S(1)} %add_convert_fusion.4), channel_id=1, source_target_pairs={{0,64},{32,96},{64,128},{96,160},{128,192},{160,224},{192,0},{224,... | collective-permute-start | bytes 1720328 | tf_op jit(solution)/shard_map/ppermute | solution.py:15
  197.1 23.3 %collective-permute-start.31 = (bf16[320,896]{1,0:T(8,128)(2,1)S(1)}, bf16[320,896]{1,0:T(8,128)(2,1)S(1)}, u32[]{:S(2)}, u32[]{:S(2)}) collective-permute-start(bf16[320,896]{1,0:T(8,128)(2,1)S(1)} %add_convert_fusion.1), channel_id=1, source_target_pairs={{0,32},{32,0},{64,96},{96,64},{128,160},{160,128},{192,224},{224,1... | collective-permute-start | bytes 1720328 | tf_op jit(solution)/shard_map/ppermute | solution.py:19
  222.6 4.2 %copy-start.12 = (f32[160,2]{0,1:T(2,128)S(1)}, f32[160,2]{0,1:T(2,128)}, u32[]{:S(2)}) copy-start(f32[160,2]{0,1:T(2,128)} %param.8) | copy-start | bytes 3844
  222.6 39.1 %all-to-all-start.1 = ((bf16[32,24,896]{2,1,0:T(8,128)(2,1)}), bf16[32,24,896]{2,1,0:T(8,128)(2,1)S(1)}, u32[]{:S(2)}, u32[]{:S(2)}) async-start(bf16[32,24,896]{2,1,0:T(8,128)(2,1)} %bitcast.16), calls=%async_computation.1 | async-start | bytes 2752512 | tf_op jit(solution)/shard_map/all_to_all | solution.py:37
